TPU v7x, 256 devices: a whole 4x4x8 slice. The times are simulated.
256 devices in a mesh: dp: 2 (over x_lo), seq: 16 (over z, core), fsdp: 8 (over x_hi, y).
Axes of the slice: x: 4 (x_hi: 2, x_lo: 2; x = x_hi * 2 + x_lo), y: 4, z: 8, core: 2. Of those that a mesh axis runs over, the one named last changes fastest.
Arguments:
- queries_raw: bfloat16 [16, 4096, 2048], P(('dp', 'fsdp'), 'seq'), parts along dimension 0, may hold values from -6 to 6
- keys_values: bfloat16 [16, 4096, 2048], P(('dp', 'fsdp'), 'seq'), parts along dimension 0, may hold values from -6 to 6
- doc_ids: int32 [16, 4096], P(('dp', 'fsdp')), parts along dimension 0, may hold values from 0 to 3, never falling along the last dimension, each value on 1 to 2048 neighbouring positions
- q_gain: float32 [128], replicated, may hold values from 0.6 to 7
- k_gain: float32 [128], replicated, may hold values from 0.6 to 7
- out_weight: bfloat16 [2048, 5376], P('fsdp'), may hold values from -0.125 to 0.125
- post_gain: float32 [5376], replicated, may hold values from 0.25 to 1.75
Outputs:
- layer_out: bfloat16 [16, 4096, 5376], P(('dp', 'fsdp'), 'seq'), parts along dimension 0
There are 2 independent parts, one for each index of `dp`. A program takes and returns all parts, laid end to end along the dimension named above; an argument that names none is the same for every part. Nothing has to cross between parts.
Inputs may be any that keep to these rules, and one draw needn't show every extreme that they name: `doc_ids`: each slab's document numbers never fall; a document has at most 2048 tokens, and one has exactly that many.
All inputs are finite; a program needn't handle non-finite values.
Results may differ from a plain program's by a relative error of at most 0.008.
The roundings to bfloat16 on the way count: a program that leaves them out, or rounds other values in their place, can miss the bound.
Values may be sent and summed in bfloat16 or wider, within the bound.
No kernel may reach another device: no remote copies, remote signals or barrier semaphores. Data moves between devices by JAX's collectives and lax.ppermute only.
A program may use at most 128 MiB of HBM per device.

v0:
```python
import math
import jax
import jax.numpy as jnp
from jax import lax
from jax.sharding import PartitionSpec as P

WINDOW = 1024
attn_scale = 168.0 ** (-0.5)
norm_eps = 1e-06


def from_behind(block, axis, distance):
    devices = range(lax.axis_size(axis))
    route = [(i - distance, i) for i in devices if i - distance in devices]
    return lax.ppermute(block, axis, route)


def doc_positions(ids):
    count = ids.shape[0]
    index = jnp.arange(count, dtype=jnp.int32)
    flags = jnp.concatenate([jnp.ones((1,), bool), ids[1:] != ids[:-1]])
    starts = lax.cummax(jnp.where(flags, index, 0), axis=0)
    return index - starts


def norm_rope(inputs, gain, positions):
    values = inputs.astype(jnp.float32)
    meansq = jnp.mean(values * values, axis=-1, keepdims=True)
    scaled = values * lax.rsqrt(meansq + norm_eps) * gain
    width = values.shape[-1]
    half = width // 2
    inverse = 10000.0 ** (-(jnp.arange(half, dtype=jnp.float32) * 2.0 / width))
    angles = positions.astype(jnp.float32)[:, None] * inverse[None, :]
    cosine = jnp.cos(angles)[:, None, :]
    sine = jnp.sin(angles)[:, None, :]
    first = scaled[..., :half]
    second = scaled[..., half:]
    rotated = jnp.concatenate(
        [first * cosine - second * sine, second * cosine + first * sine], axis=-1
    )
    return rotated.astype(jnp.bfloat16)


def on_device(queries_raw, keys_values, doc_ids, q_gain, k_gain, out_weight, post_gain):
    tokens = queries_raw.shape[1]
    head_dim = q_gain.shape[0]
    features = queries_raw.shape[2]
    heads = features // head_dim
    kv_cols = keys_values.shape[2] // 2
    kv_heads = kv_cols // head_dim
    group = heads // kv_heads
    seq_index = lax.axis_index("seq")
    begin = seq_index * tokens
    ids_all = doc_ids[0]
    positions = lax.dynamic_slice_in_dim(doc_positions(ids_all), begin, tokens, 0)
    queries = norm_rope(queries_raw[0].reshape(tokens, heads, head_dim), q_gain, positions)
    queries = queries.reshape(tokens, kv_heads, group, head_dim)
    raw_pairs = keys_values[0]
    keys = norm_rope(raw_pairs[:, :kv_cols].reshape(tokens, kv_heads, head_dim), k_gain, positions)
    local = jnp.concatenate([keys.reshape(tokens, kv_cols), raw_pairs[:, kv_cols:]], axis=1)
    reach = (WINDOW - 2) // tokens + 1
    pieces = []
    for offset in range(reach, 0, -1):
        pieces.append(from_behind(local, "seq", offset))
    pieces.append(local)
    joined = jnp.concatenate(pieces, axis=0)
    span = (reach + 1) * tokens
    ids_pad = jnp.concatenate([jnp.full((reach * tokens,), -1, jnp.int32), ids_all])
    key_ids = lax.dynamic_slice_in_dim(ids_pad, begin, span, 0)
    query_ids = lax.dynamic_slice_in_dim(ids_all, begin, tokens, 0)
    key_rows = joined[:, :kv_cols].reshape(span, kv_heads, head_dim)
    value_rows = joined[:, kv_cols:].reshape(span, kv_heads, head_dim)
    block = math.gcd(tokens, 512)
    relative = (
        reach * tokens
        + jnp.arange(block, dtype=jnp.int32)[:, None]
        - jnp.arange(span, dtype=jnp.int32)[None, :]
    )
    allowed = (relative >= 0) & (relative < WINDOW) & (query_ids[0:block, None] == key_ids[None, :])
    scores = (
        jnp.einsum("tkgd,ukd->kgtu", queries, key_rows, preferred_element_type=jnp.float32)
        * attn_scale
    )
    scores = jnp.where(allowed[None, None], scores, -jnp.inf)
    top = jnp.max(scores, axis=-1, keepdims=True)
    expd = jnp.exp(scores - top)
    total = jnp.sum(expd, axis=-1, keepdims=True)
    probs = (expd / total).astype(jnp.bfloat16)
    mixed = jnp.einsum("kgtu,ukd->tkgd", probs, value_rows, preferred_element_type=jnp.float32)
    outputs = mixed.reshape(block, features).astype(jnp.bfloat16)
    n_fsdp = lax.axis_size("fsdp")
    n_seq = lax.axis_size("seq")
    each = out_weight.shape[0] // n_seq
    mine = lax.dynamic_slice_in_dim(out_weight, begin // tokens * each, each, 0)
    arranged = (
        outputs.reshape(tokens, n_fsdp, n_seq, each).transpose(0, 2, 1, 3).reshape(tokens, features)
    )
    partial_rows = lax.all_gather(mine, "fsdp", axis=0, tiled=True)
    all_rows = lax.all_gather(partial_rows, "seq", axis=0, tiled=True)
    projected = jnp.dot(arranged, all_rows, preferred_element_type=jnp.float32)
    meansq = jnp.mean(projected * projected, axis=-1, keepdims=True)
    result = (projected * lax.rsqrt(meansq + norm_eps) * post_gain).astype(jnp.bfloat16)
    return result[None]


def solution(mesh):
    in_specs = (
        P(("dp", "fsdp"), "seq", None),
        P(("dp", "fsdp"), "seq", None),
        P(("dp", "fsdp"), None),
        P(),
        P(),
        P("fsdp", None),
        P(),
    )
    out_specs = P(("dp", "fsdp"), "seq", None)
    return jax.shard_map(
        on_device, mesh=mesh, in_specs=in_specs, out_specs=out_specs, check_vma=False
    )
```

profile of v0, /device:TPU:64, one launch (start us, length us, event | category | flops | bytes accessed | tf_op | source)
XLA Modules:
  0.0 324.0 jit_solution(14192368447268685597)
XLA Ops:
  6.5 0.0 copy-start
  6.5 0.0 all-gather.3.cloned.1.call-start
  6.5 1.8 copy-done
  8.3 0.7 constant_dynamic-slice_fusion
  9.0 0.0 all-gather.3.cloned.1.call-update
  9.0 0.0 all-gather.5.cloned.1.call-start
  9.1 56.5 %all-gather.3.cloned.1.call-done = bf16[128,5376]{1,0:T(8,128)(2,1)} async-done(((bf16[16,5376]{1,0:T(8,128)(2,1)}), bf16[128,5376]{1,0:T(8,128)(2,1)}) %all-gather.3.cloned.1.call-update) | async-done | bytes 1376272 | tf_op jit(solution)/shard_map/all_gather | solution.py:98
  65.6 0.0 all-gather.5.cloned.1.call-update
  65.6 0.9 compare_reduce_fusion
  66.5 0.1 add_select_fusion
  66.6 0.3 reduce-window.9
  66.9 0.1 slice.53
  67.0 0.1 reduce-window.12
  67.0 1.5 copy.26
  68.6 0.1 slice_reduce_fusion
  68.7 0.1 maximum_bitcast_fusion
  68.8 0.1 fusion.11
  68.9 0.1 fusion.9
  69.0 0.3 multiply_cosine_fusion
  69.3 0.0 copy-done.5
  69.3 0.2 fusion.10
  69.5 0.0 copy-start.2
  69.5 0.1 subtract_convert_fusion.1
  69.7 1.0 pad_maximum_fusion
  70.7 5.7 %collective-permute-start = (bf16[256,2048]{0,1:T(8,128)(2,1)}, bf16[256,2048]{0,1:T(8,128)(2,1)}, u32[]{:S(2)}, u32[]{:S(2)}) collective-permute-start(bf16[256,2048]{0,1:T(8,128)(2,1)} %pad_maximum_fusion), channel_id=1, source_target_pairs={{0,32},{8,40},{16,48},{24,56},{32,64},{40,72},{48,80},{56,88},{64,... | collective-permute-start | bytes 3145736 | tf_op jit(solution)/shard_map/ppermute | solution.py:15
  76.4 1.9 collective-permute-start.1
  78.3 2.6 collective-permute-start.2
  80.9 2.5 collective-permute-start.3
  83.4 0.1 copy.29
  83.5 0.1 copy.30
  83.6 0.0 copy-done.2
  83.6 0.2 convert_bitcast_fusion
  83.8 0.4 copy.41
  84.2 0.6 multiply_reduce_fusion.1
  84.9 0.1 copy.27
  84.9 0.6 add_rsqrt_fusion
  85.5 0.8 copy.28
  86.4 1.4 multiply_multiply_fusion
  87.8 0.8 subtract_convert_fusion
  88.6 0.0 copy-start.3
  88.6 1.3 copy.31
  89.9 1.2 copy.32
  91.1 0.0 copy-done.3
  91.1 0.1 pad_dynamic-slice_fusion
  91.2 0.5 fusion.8
  91.7 48.3 %collective-permute-done = bf16[256,2048]{0,1:T(8,128)(2,1)} collective-permute-done((bf16[256,2048]{0,1:T(8,128)(2,1)}, bf16[256,2048]{0,1:T(8,128)(2,1)}, u32[]{:S(2)}, u32[]{:S(2)}) %collective-permute-start) | collective-permute-done | bytes 1048608 | tf_op jit(solution)/shard_map/ppermute | solution.py:15
  140.0 1.3 constant_dynamic-update-slice_fusion.4
  141.3 59.7 %collective-permute-done.1 = bf16[256,2048]{0,1:T(8,128)(2,1)} collective-permute-done((bf16[256,2048]{0,1:T(8,128)(2,1)}, bf16[256,2048]{0,1:T(8,128)(2,1)}, u32[]{:S(2)}, u32[]{:S(2)}) %collective-permute-start.1) | collective-permute-done | bytes 1048608 | tf_op jit(solution)/shard_map/ppermute | solution.py:15
  201.0 1.3 constant_dynamic-update-slice_fusion.3
  202.3 43.6 %collective-permute-done.2 = bf16[256,2048]{0,1:T(8,128)(2,1)} collective-permute-done((bf16[256,2048]{0,1:T(8,128)(2,1)}, bf16[256,2048]{0,1:T(8,128)(2,1)}, u32[]{:S(2)}, u32[]{:S(2)}) %collective-permute-start.2) | collective-permute-done | bytes 1048608 | tf_op jit(solution)/shard_map/ppermute | solution.py:15
  245.9 1.3 constant_dynamic-update-slice_fusion.2
  247.2 30.1 %collective-permute-done.3 = bf16[256,2048]{0,1:T(8,128)(2,1)} collective-permute-done((bf16[256,2048]{0,1:T(8,128)(2,1)}, bf16[256,2048]{0,1:T(8,128)(2,1)}, u32[]{:S(2)}, u32[]{:S(2)}) %collective-permute-start.3) | collective-permute-done | bytes 1048608 | tf_op jit(solution)/shard_map/ppermute | solution.py:15
  277.4 1.3 constant_dynamic-update-slice_fusion.1
  278.7 0.1 constant_dynamic-update-slice_fusion
  278.8 1.8 fusion.19
  280.6 8.7 %exponential_reduce_fusion = f32[8,2,256]{2,1,0:T(2,128)S(1)} fusion(bf16[1280,8,128,1]{0,2,3,1:T(8,128)(2,1)S(1)} %bitcast.63, pred[256,1280]{0,1:T(8,128)(4,1)S(1)} %fusion.8, bf16[256,8,2,64]{3,0,2,1:T(8,128)(2,1)} %bitcast.68, bf16[256,8,2,64]{3,0,2,1:T(8,128)(2,1)} %bitcast.66), kind=kOutput, calls=%fused_computation.4 | convolution fusion | flops 1365247232 | bytes 4014080 | tf_op jit(solution)/shard_map/sub | solution.py:86
  289.3 13.2 %fusion.4 = bf16[8,128,2,256]{3,1,2,0:T(8,128)(2,1)} fusion(bf16[1280,8,128,1]{0,2,3,1:T(8,128)(2,1)} %bitcast.65, f32[8,2,256]{2,1,0:T(2,128)S(1)} %exponential_reduce_fusion, bf16[1280,8,128,1]{0,2,3,1:T(8,128)(2,1)S(1)} %bitcast.64, pred[256,1280]{0,1:T(8,128)(4,1)S(1)} %fusion.8, bf16[256,8,2,64]{3,0,2,1:T(8,128)(2,1)} %bitcast.69, ...), kind=kOutput, calls=%fused_computation.14 | convolution fusion | flops 2713195776 | bytes 7684096 | tf_op jit(solution)/shard_map/kgtu,ukd->tkgd/dot_general | solution.py:89
  302.5 1.3 copy.35
  303.8 0.0 all-gather.5.cloned.1.call-done
  303.9 0.0 copy-start.4
  303.9 10.9 %multiply_reduce_fusion = (f32[256]{0:T(256)S(1)}, f32[256,5376]{1,0:T(8,128)S(1)}) fusion(bf16[256,2048]{0,1:T(8,128)(2,1)S(1)} %bitcast.62, bf16[2048,5376]{1,0:T(8,128)(2,1)} %all-gather.5.cloned.1.call-done), kind=kOutput, calls=%fused_computation.7 | convolution fusion | flops 5639897088 | bytes 28574720 | tf_op jit(solution)/shard_map/dot_general | solution.py:100
  314.8 0.0 copy-start.1
  314.9 2.1 fusion.3
  317.0 0.2 copy-done.1
  (9 shorter events, 0.1 us)
Async XLA Ops:
  6.5 1.8 copy-start
  6.5 59.1 %all-gather.3.cloned.1.call-start = ((), (), s32[]{:S(2)}) async-start(), calls=%async_computation | async-start | bytes 1548288 | tf_op jit(solution)/shard_map/all_gather | solution.py:98
  9.0 294.8 %all-gather.5.cloned.1.call-start = ((), (), s32[]{:S(2)}) async-start(), calls=%async_computation.1 | async-start | bytes 23396352 | tf_op jit(solution)/shard_map/all_gather | solution.py:99
  65.6 3.7 %copy-start.5 = (f32[128]{0:T(128)S(1)}, f32[128]{0:T(128)}, u32[]{:S(2)}) copy-start(f32[128]{0:T(128)} %param.11) | copy-start | bytes 1540
  69.5 14.1 %copy-start.2 = (bf16[1,256,2048]{2,1,0:T(8,128)(2,1)S(1)}, bf16[1,256,2048]{2,1,0:T(8,128)(2,1)}, u32[]{:S(2)}) copy-start(bf16[1,256,2048]{2,1,0:T(8,128)(2,1)} %param.7) | copy-start | bytes 3145732
  70.7 69.2 %collective-permute-start = (bf16[256,2048]{0,1:T(8,128)(2,1)}, bf16[256,2048]{0,1:T(8,128)(2,1)}, u32[]{:S(2)}, u32[]{:S(2)}) collective-permute-start(bf16[256,2048]{0,1:T(8,128)(2,1)} %pad_maximum_fusion), channel_id=1, source_target_pairs={{0,32},{8,40},{16,48},{24,56},{32,64},{40,72},{48,80},{56,88},{64,... | collective-permute-start | bytes 3145736 | tf_op jit(solution)/shard_map/ppermute | solution.py:15
  76.4 124.6 %collective-permute-start.1 = (bf16[256,2048]{0,1:T(8,128)(2,1)}, bf16[256,2048]{0,1:T(8,128)(2,1)}, u32[]{:S(2)}, u32[]{:S(2)}) collective-permute-start(bf16[256,2048]{0,1:T(8,128)(2,1)} %pad_maximum_fusion), channel_id=1, source_target_pairs={{0,24},{8,32},{16,40},{24,48},{32,56},{40,64},{48,72},{56,80},{64,... | collective-permute-start | bytes 3145736 | tf_op jit(solution)/shard_map/ppermute | solution.py:15
  78.3 167.6 %collective-permute-start.2 = (bf16[256,2048]{0,1:T(8,128)(2,1)}, bf16[256,2048]{0,1:T(8,128)(2,1)}, u32[]{:S(2)}, u32[]{:S(2)}) collective-permute-start(bf16[256,2048]{0,1:T(8,128)(2,1)} %pad_maximum_fusion), channel_id=1, source_target_pairs={{0,16},{8,24},{16,32},{24,40},{32,48},{40,56},{48,64},{56,72},{64,... | collective-permute-start | bytes 3145736 | tf_op jit(solution)/shard_map/ppermute | solution.py:15
  80.9 196.5 %collective-permute-start.3 = (bf16[256,2048]{0,1:T(8,128)(2,1)}, bf16[256,2048]{0,1:T(8,128)(2,1)}, u32[]{:S(2)}, u32[]{:S(2)}) collective-permute-start(bf16[256,2048]{0,1:T(8,128)(2,1)} %pad_maximum_fusion), channel_id=1, source_target_pairs={{0,8},{8,16},{16,24},{24,32},{32,40},{40,48},{48,56},{56,64},{64,7... | collective-permute-start | bytes 3145736 | tf_op jit(solution)/shard_map/ppermute | solution.py:15
  88.6 2.5 copy-start.3
  303.9 11.0 %copy-start.4 = (f32[5376]{0:T(1024)S(1)}, f32[5376]{0:T(1024)}, u32[]{:S(2)}) copy-start(f32[5376]{0:T(1024)} %param.13) | copy-start | bytes 64516
  314.8 2.3 copy-start.1
Sparse Core Ops, SparseCore 0:
  9.9 55.6 all-gather.2
  67.4 225.4 all-gather.4
where the time goes:
time: 325 us; the launch traced here: 324 us
  waiting for transfers between devices  238 us (73%)
  matrix products  32.8 us (10%)
  local copies, waits for them, and re-layouts  16.8 us (5%)
  between operations  13.7 us (4%)
  starting transfers between devices  12.7 us (4%)
  other arithmetic  9.65 us (3%)
    ppermute x4, waiting for transfers between devices, from_behind(): return lax.ppermute(block, axis, route)  182 us
    all_gather x1, waiting for transfers between devices, on_device(): partial_rows = lax.all_gather(mine, 'fsdp', axis=0, tiled=True)  56.5 us
    dot_general x1, matrix products, on_device(): jnp.einsum('kgtu,ukd->tkgd', probs, value_rows, preferred_element_type=jn...  13.2 us
    ppermute x4, starting transfers between devices, from_behind(): return lax.ppermute(block, axis, route)  12.6 us
    dot_general x1, matrix products, on_device(): projected = jnp.dot(arranged, all_rows, preferred_element_type=jnp.float32)  10.9 us
    unnamed x18, local copies, waits for them, and re-layouts  9.05 us
    sub x1, matrix products, on_device(): expd = jnp.exp(scores - top)  8.73 us
  transfers between devices with their start and end apart: 6, of which 5 were waited for; matrix products, arithmetic and copies ran while one was open for 13% of the time, Pallas kernels for 0%

commit v1 on v0

--- a/solution.py
+++ b/solution.py
@@ -1,12 +1,38 @@
+import functools
 import math
 import jax
 import jax.numpy as jnp
 from jax import lax
 from jax.sharding import PartitionSpec as P
+from jax.lax import axis_index, axis_size, ppermute
 
 WINDOW = 1024
 attn_scale = 168.0 ** (-0.5)
 norm_eps = 1e-06
+
+
+def refer_regions(field, across):
+    left_arr = axis_size(across)
+    raw_out = axis_index(across)
+    odd, state_next, oldest = (left_arr, raw_out, field.shape[0])
+    shelf = tuple(((at, (at + 1) % odd) for at in range(odd)))
+    gallery = tuple(((at, (at - 1) % odd) for at in range(odd)))
+    high = jnp.zeros((*field.shape[:0], odd * oldest, *field.shape[1:]), field.dtype)
+    high = lax.dynamic_update_slice_in_dim(high, field, state_next * oldest, axis=0)
+    clean = h_now = field
+    ready = odd // 2
+    for k in [*range(1, ready + 1)]:
+        clean = ppermute(clean, across, shelf)
+        high = lax.dynamic_update_slice_in_dim(high, clean, (state_next - k) % odd * oldest, axis=0)
+        if k < odd - ready:
+            h_now = ppermute(h_now, across, gallery)
+            high = lax.dynamic_update_slice_in_dim(
+                high, h_now, (state_next + k) % odd * oldest, axis=0
+            )
+    return high
+
+
+draw_bench = functools.partial(refer_regions, across="seq")
 
 
 def from_behind(block, axis, distance):
@@ -96,7 +122,7 @@
         outputs.reshape(tokens, n_fsdp, n_seq, each).transpose(0, 2, 1, 3).reshape(tokens, features)
     )
     partial_rows = lax.all_gather(mine, "fsdp", axis=0, tiled=True)
-    all_rows = lax.all_gather(partial_rows, "seq", axis=0, tiled=True)
+    all_rows = draw_bench(partial_rows)
     projected = jnp.dot(arranged, all_rows, preferred_element_type=jnp.float32)
     meansq = jnp.mean(projected * projected, axis=-1, keepdims=True)
     result = (projected * lax.rsqrt(meansq + norm_eps) * post_gain).astype(jnp.bfloat16)

time: 325 us -> 328 us (level)
  the two profiles are of different devices: /device:TPU:64 before, /device:TPU:140 now
where the time goes in v1:
time: 328 us; the launch traced here: 327 us
  waiting for transfers between devices  191 us (58%)
  local copies, waits for them, and re-layouts  46.1 us (14%)
  matrix products  32.9 us (10%)
  starting transfers between devices  30.8 us (9%)
  between operations  14 us (4%)
  other arithmetic  12.5 us (4%)
    ppermute x8, waiting for transfers between devices, refer_regions(): clean = ppermute(clean, across, shelf)  95.7 us
    ppermute x4, waiting for transfers between devices, from_behind(): return lax.ppermute(block, axis, route)  95.2 us
    ppermute x7, starting transfers between devices, refer_regions(): h_now = ppermute(h_now, across, gallery)  20.7 us
    dot_general x1, matrix products, on_device(): jnp.einsum('kgtu,ukd->tkgd', probs, value_rows, preferred_element_type=jn...  13.2 us
    dot_general x1, matrix products, on_device(): projected = jnp.dot(arranged, all_rows, preferred_element_type=jnp.float32)  11 us
    dynamic_update_slice x8, local copies, waits for them, and re-layouts, refer_regions(): lax.dynamic_update_slice_in_dim(high, clean, (state_next - k) % odd * old...  10.9 us
    ppermute x4, starting transfers between devices, from_behind(): return lax.ppermute(block, axis, route)  10.1 us
    dynamic_update_slice x7, local copies, waits for them, and re-layouts, refer_regions(): lax.dynamic_update_slice_in_dim(high, h_now, (state_next + k) % odd * old...  9.7 us
  transfers between devices with their start and end apart: 20, of which 11 were waited for; matrix products, arithmetic and copies ran while one was open for 21% of the time, Pallas kernels for 0%

profile of v1, /device:TPU:140, one launch (start us, length us, event | category | flops | bytes accessed | tf_op | source)
XLA Modules:
  0.0 327.2 jit_solution(16188892963323051119)
XLA Ops:
  6.6 2.4 copy.26
  9.0 1.2 fusion.9
  10.1 1.1 slice.56
  11.2 0.9 compare_reduce_fusion
  13.2 1.2 fusion.10
  14.7 0.8 copy-done.2
  15.5 1.0 pad_maximum_fusion
  16.5 3.4 %collective-permute-start = (bf16[256,2048]{0,1:T(8,128)(2,1)}, bf16[256,2048]{0,1:T(8,128)(2,1)}, u32[]{:S(2)}, u32[]{:S(2)}) collective-permute-start(bf16[256,2048]{0,1:T(8,128)(2,1)} %pad_maximum_fusion), channel_id=1, source_target_pairs={{0,32},{8,40},{16,48},{24,56},{32,64},{40,72},{48,80},{56,88},{64,... | collective-permute-start | bytes 3145736 | tf_op jit(solution)/shard_map/ppermute | solution.py:41
  19.9 2.1 collective-permute-start.1
  22.0 2.8 collective-permute-start.2
  24.8 1.9 collective-permute-start.3
  26.7 0.7 constant_dynamic-slice_fusion
  27.9 1.5 convert_bitcast_fusion
  29.8 0.6 multiply_reduce_fusion.1
  30.6 0.9 multiply_multiply_fusion
  31.5 0.8 subtract_convert_fusion
  32.2 1.3 copy.31
  33.5 1.2 copy.32
  34.9 1.2 fusion.8
  36.1 12.8 %collective-permute-done = bf16[256,2048]{0,1:T(8,128)(2,1)} collective-permute-done((bf16[256,2048]{0,1:T(8,128)(2,1)}, bf16[256,2048]{0,1:T(8,128)(2,1)}, u32[]{:S(2)}, u32[]{:S(2)}) %collective-permute-start) | collective-permute-done | bytes 1048608 | tf_op jit(solution)/shard_map/ppermute | solution.py:41
  48.8 1.3 constant_dynamic-update-slice_fusion.4
  50.1 50.6 %collective-permute-done.1 = bf16[256,2048]{0,1:T(8,128)(2,1)} collective-permute-done((bf16[256,2048]{0,1:T(8,128)(2,1)}, bf16[256,2048]{0,1:T(8,128)(2,1)}, u32[]{:S(2)}, u32[]{:S(2)}) %collective-permute-start.1) | collective-permute-done | bytes 1048608 | tf_op jit(solution)/shard_map/ppermute | solution.py:41
  100.7 1.3 constant_dynamic-update-slice_fusion.3
  102.0 22.5 %collective-permute-done.2 = bf16[256,2048]{0,1:T(8,128)(2,1)} collective-permute-done((bf16[256,2048]{0,1:T(8,128)(2,1)}, bf16[256,2048]{0,1:T(8,128)(2,1)}, u32[]{:S(2)}, u32[]{:S(2)}) %collective-permute-start.2) | collective-permute-done | bytes 1048608 | tf_op jit(solution)/shard_map/ppermute | solution.py:41
  124.5 1.3 constant_dynamic-update-slice_fusion.2
  125.8 9.4 %collective-permute-done.3 = bf16[256,2048]{0,1:T(8,128)(2,1)} collective-permute-done((bf16[256,2048]{0,1:T(8,128)(2,1)}, bf16[256,2048]{0,1:T(8,128)(2,1)}, u32[]{:S(2)}, u32[]{:S(2)}) %collective-permute-start.3) | collective-permute-done | bytes 1048608 | tf_op jit(solution)/shard_map/ppermute | solution.py:41
  135.2 1.3 constant_dynamic-update-slice_fusion.1
  136.6 1.8 fusion.19
  138.4 3.0 collective-permute-start.5
  141.3 8.7 %exponential_reduce_fusion = f32[8,2,256]{2,1,0:T(2,128)S(1)} fusion(bf16[1280,8,128,1]{0,2,3,1:T(8,128)(2,1)S(1)} %bitcast.63, pred[256,1280]{0,1:T(8,128)(4,1)S(1)} %copy-done.5, bf16[256,8,2,64]{3,0,2,1:T(8,128)(2,1)} %bitcast.68, bf16[256,8,2,64]{3,0,2,1:T(8,128)(2,1)} %bitcast.66), kind=kOutput, calls=%fused_computation.4 | convolution fusion | flops 1365247232 | bytes 4014080 | tf_op jit(solution)/shard_map/sub | solution.py:112
  150.1 13.2 %fusion.4 = bf16[8,128,2,256]{3,1,2,0:T(8,128)(2,1)} fusion(bf16[1280,8,128,1]{0,2,3,1:T(8,128)(2,1)} %bitcast.65, f32[8,2,256]{2,1,0:T(2,128)S(1)} %exponential_reduce_fusion, bf16[1280,8,128,1]{0,2,3,1:T(8,128)(2,1)S(1)} %bitcast.64, pred[256,1280]{0,1:T(8,128)(4,1)S(1)} %copy-done.5, bf16[256,8,2,64]{3,0,2,1:T(8,128)(2,1)} %bitcast.69, ...), kind=kOutput, calls=%fused_computation.14 | convolution fusion | flops 2713195776 | bytes 7684096 | tf_op jit(solution)/shard_map/kgtu,ukd->tkgd/dot_general | solution.py:115
  163.3 1.3 copy.35
  164.6 7.5 %broadcast_in_dim.19 = bf16[2048,5376]{1,0:T(8,128)(2,1)} broadcast(bf16[]{:T(256)} %constant.147.clone.1), dimensions={} | broadcast | bytes 22020098 | tf_op jit(solution)/shard_map/broadcast_in_dim | solution.py:20
  172.1 1.2 constant_dynamic-update-slice_fusion.20
  173.2 3.0 collective-permute-start.7
  176.2 2.5 constant_dynamic-update-slice_fusion.19
  178.7 2.6 constant_dynamic-update-slice_fusion.18
  181.3 11.1 %collective-permute-done.6 = bf16[128,5376]{1,0:T(8,128)(2,1)S(1)} collective-permute-done((bf16[128,5376]{1,0:T(8,128)(2,1)}, bf16[128,5376]{1,0:T(8,128)(2,1)S(1)}, u32[]{:S(2)}, u32[]{:S(2)}) %collective-permute-start.6) | collective-permute-done | bytes 1376288 | tf_op jit(solution)/shard_map/ppermute | solution.py:25
  192.4 3.0 collective-permute-start.9
  195.3 1.3 constant_dynamic-update-slice_fusion.17
  196.6 1.2 constant_dynamic-update-slice_fusion.16
  197.8 13.6 %collective-permute-done.8 = bf16[128,5376]{1,0:T(8,128)(2,1)S(1)} collective-permute-done((bf16[128,5376]{1,0:T(8,128)(2,1)S(1)}, bf16[128,5376]{1,0:T(8,128)(2,1)S(1)}, u32[]{:S(2)}, u32[]{:S(2)}) %collective-permute-start.8) | collective-permute-done | bytes 1376288 | tf_op jit(solution)/shard_map/ppermute | solution.py:25
  211.3 3.0 collective-permute-start.11
  214.3 1.2 constant_dynamic-update-slice_fusion.15
  215.5 1.2 constant_dynamic-update-slice_fusion.14
  216.6 13.6 %collective-permute-done.10 = bf16[128,5376]{1,0:T(8,128)(2,1)S(1)} collective-permute-done((bf16[128,5376]{1,0:T(8,128)(2,1)S(1)}, bf16[128,5376]{1,0:T(8,128)(2,1)S(1)}, u32[]{:S(2)}, u32[]{:S(2)}) %collective-permute-start.10) | collective-permute-done | bytes 1376288 | tf_op jit(solution)/shard_map/ppermute | solution.py:25
  230.3 3.0 collective-permute-start.13
  233.2 1.2 constant_dynamic-update-slice_fusion.13
  234.4 1.2 constant_dynamic-update-slice_fusion.12
  235.6 13.6 %collective-permute-done.12 = bf16[128,5376]{1,0:T(8,128)(2,1)S(1)} collective-permute-done((bf16[128,5376]{1,0:T(8,128)(2,1)S(1)}, bf16[128,5376]{1,0:T(8,128)(2,1)S(1)}, u32[]{:S(2)}, u32[]{:S(2)}) %collective-permute-start.12) | collective-permute-done | bytes 1376288 | tf_op jit(solution)/shard_map/ppermute | solution.py:25
  249.2 3.0 collective-permute-start.15
  252.2 1.2 constant_dynamic-update-slice_fusion.11
  253.3 1.2 constant_dynamic-update-slice_fusion.10
  254.6 13.6 %collective-permute-done.14 = bf16[128,5376]{1,0:T(8,128)(2,1)S(1)} collective-permute-done((bf16[128,5376]{1,0:T(8,128)(2,1)S(1)}, bf16[128,5376]{1,0:T(8,128)(2,1)S(1)}, u32[]{:S(2)}, u32[]{:S(2)}) %collective-permute-start.14) | collective-permute-done | bytes 1376288 | tf_op jit(solution)/shard_map/ppermute | solution.py:25
  268.2 3.0 collective-permute-start.17
  271.1 1.2 constant_dynamic-update-slice_fusion.9
  272.3 1.2 constant_dynamic-update-slice_fusion.8
  273.5 13.6 %collective-permute-done.16 = bf16[128,5376]{1,0:T(8,128)(2,1)S(1)} collective-permute-done((bf16[128,5376]{1,0:T(8,128)(2,1)S(1)}, bf16[128,5376]{1,0:T(8,128)(2,1)S(1)}, u32[]{:S(2)}, u32[]{:S(2)}) %collective-permute-start.16) | collective-permute-done | bytes 1376288 | tf_op jit(solution)/shard_map/ppermute | solution.py:25
  287.1 1.2 constant_dynamic-update-slice_fusion.7
  288.3 1.2 constant_dynamic-update-slice_fusion.6
  289.4 16.6 %collective-permute-done.18 = bf16[128,5376]{1,0:T(8,128)(2,1)S(1)} collective-permute-done((bf16[128,5376]{1,0:T(8,128)(2,1)S(1)}, bf16[128,5376]{1,0:T(8,128)(2,1)S(1)}, u32[]{:S(2)}, u32[]{:S(2)}) %collective-permute-start.18) | collective-permute-done | bytes 1376288 | tf_op jit(solution)/shard_map/ppermute | solution.py:25
  306.0 1.2 constant_dynamic-update-slice_fusion.5
  307.3 11.0 %multiply_reduce_fusion = (f32[256]{0:T(256)S(1)}, f32[256,5376]{1,0:T(8,128)S(1)}) fusion(bf16[256,2048]{0,1:T(8,128)(2,1)S(1)} %bitcast.62, bf16[2048,5376]{1,0:T(8,128)(2,1)} %constant_dynamic-update-slice_fusion.5), kind=kOutput, calls=%fused_computation.7 | convolution fusion | flops 5639897088 | bytes 28574720 | tf_op jit(solution)/shard_map/dot_general | solution.py:126
  318.2 2.1 fusion.3
  (59 shorter events, 2.3 us)
Async XLA Ops:
  6.5 20.2 %copy-start = (bf16[256,5376]{1,0:T(8,128)(2,1)S(1)}, bf16[256,5376]{1,0:T(8,128)(2,1)}, u32[]{:S(2)}) copy-start(bf16[256,5376]{1,0:T(8,128)(2,1)} %param.12) | copy-start | bytes 8257540
  6.5 131.8 %all-gather.2.cloned.1.call-start = ((), (), s32[]{:S(2)}) async-start(), calls=%async_computation | async-start | bytes 1548288 | tf_op jit(solution)/shard_map/all_gather | solution.py:124
  14.7 0.8 copy-start.2
  16.5 32.3 %collective-permute-start = (bf16[256,2048]{0,1:T(8,128)(2,1)}, bf16[256,2048]{0,1:T(8,128)(2,1)}, u32[]{:S(2)}, u32[]{:S(2)}) collective-permute-start(bf16[256,2048]{0,1:T(8,128)(2,1)} %pad_maximum_fusion), channel_id=1, source_target_pairs={{0,32},{8,40},{16,48},{24,56},{32,64},{40,72},{48,80},{56,88},{64,... | collective-permute-start | bytes 3145736 | tf_op jit(solution)/shard_map/ppermute | solution.py:41
  19.9 80.8 %collective-permute-start.1 = (bf16[256,2048]{0,1:T(8,128)(2,1)}, bf16[256,2048]{0,1:T(8,128)(2,1)}, u32[]{:S(2)}, u32[]{:S(2)}) collective-permute-start(bf16[256,2048]{0,1:T(8,128)(2,1)} %pad_maximum_fusion), channel_id=1, source_target_pairs={{0,24},{8,32},{16,40},{24,48},{32,56},{40,64},{48,72},{56,80},{64,... | collective-permute-start | bytes 3145736 | tf_op jit(solution)/shard_map/ppermute | solution.py:41
  22.0 102.5 %collective-permute-start.2 = (bf16[256,2048]{0,1:T(8,128)(2,1)}, bf16[256,2048]{0,1:T(8,128)(2,1)}, u32[]{:S(2)}, u32[]{:S(2)}) collective-permute-start(bf16[256,2048]{0,1:T(8,128)(2,1)} %pad_maximum_fusion), channel_id=1, source_target_pairs={{0,16},{8,24},{16,32},{24,40},{32,48},{40,56},{48,64},{56,72},{64,... | collective-permute-start | bytes 3145736 | tf_op jit(solution)/shard_map/ppermute | solution.py:41
  24.8 110.4 %collective-permute-start.3 = (bf16[256,2048]{0,1:T(8,128)(2,1)}, bf16[256,2048]{0,1:T(8,128)(2,1)}, u32[]{:S(2)}, u32[]{:S(2)}) collective-permute-start(bf16[256,2048]{0,1:T(8,128)(2,1)} %pad_maximum_fusion), channel_id=1, source_target_pairs={{0,8},{8,16},{16,24},{24,32},{32,40},{40,48},{48,56},{56,64},{64,7... | collective-permute-start | bytes 3145736 | tf_op jit(solution)/shard_map/ppermute | solution.py:41
  27.6 3.0 copy-start.8
  31.4 3.3 %copy-start.6 = (s32[1,4096]{1,0:T(1,128)S(1)}, s32[1,4096]{1,0:T(1,128)}, u32[]{:S(2)}) copy-start(s32[1,4096]{1,0:T(1,128)} %param.9) | copy-start | bytes 49156
  33.5 102.9 %copy-start.3 = (bf16[256,8,128]{0,2,1:T(8,128)(2,1)S(1)}, bf16[256,8,128]{0,2,1:T(8,128)(2,1)}, u32[]{:S(2)}) copy-start(bf16[256,8,128]{0,2,1:T(8,128)(2,1)} %copy-done.2) | copy-start | bytes 1572868
  136.5 4.8 %copy-start.5 = (pred[256,1280]{0,1:T(8,128)(4,1)S(1)}, pred[256,1280]{0,1:T(8,128)(4,1)}, u32[]{:S(2)}) copy-start(pred[256,1280]{0,1:T(8,128)(4,1)} %fusion.8) | copy-start | bytes 983044
  138.4 34.8 %collective-permute-start.4 = (bf16[128,5376]{1,0:T(8,128)(2,1)}, bf16[128,5376]{1,0:T(8,128)(2,1)}, u32[]{:S(2)}, u32[]{:S(2)}) collective-permute-start(bf16[128,5376]{1,0:T(8,128)(2,1)} %all-gather.2.cloned.1.call-done), channel_id=1, source_target_pairs={{0,8},{8,16},{16,24},{24,32},{32,40},{40,48},{48,56},{56,64},{64,7... | collective-permute-start | bytes 4128776 | tf_op jit(solution)/shard_map/ppermute | solution.py:25
  138.4 34.8 %collective-permute-start.5 = (bf16[128,5376]{1,0:T(8,128)(2,1)}, bf16[128,5376]{1,0:T(8,128)(2,1)}, u32[]{:S(2)}, u32[]{:S(2)}) collective-permute-start(bf16[128,5376]{1,0:T(8,128)(2,1)} %all-gather.2.cloned.1.call-done), channel_id=1, source_target_pairs={{0,120},{8,0},{16,8},{24,16},{32,24},{40,32},{48,40},{56,48},{64,5... | collective-permute-start | bytes 4128776 | tf_op jit(solution)/shard_map/ppermute | solution.py:28
  164.6 7.5 %copy-start.4 = (bf16[128,5376]{1,0:T(8,128)(2,1)S(1)}, bf16[128,5376]{1,0:T(8,128)(2,1)}, u32[]{:S(2)}) copy-start(bf16[128,5376]{1,0:T(8,128)(2,1)} %all-gather.2.cloned.1.call-done) | copy-start | bytes 4128772
  173.2 19.2 %collective-permute-start.6 = (bf16[128,5376]{1,0:T(8,128)(2,1)}, bf16[128,5376]{1,0:T(8,128)(2,1)S(1)}, u32[]{:S(2)}, u32[]{:S(2)}) collective-permute-start(bf16[128,5376]{1,0:T(8,128)(2,1)} %collective-permute-done.4), channel_id=1, source_target_pairs={{0,8},{8,16},{16,24},{24,32},{32,40},{40,48},{48,56},{56,64},{64,7... | collective-permute-start | bytes 4128776 | tf_op jit(solution)/shard_map/ppermute | solution.py:25
  173.2 19.2 %collective-permute-start.7 = (bf16[128,5376]{1,0:T(8,128)(2,1)}, bf16[128,5376]{1,0:T(8,128)(2,1)S(1)}, u32[]{:S(2)}, u32[]{:S(2)}) collective-permute-start(bf16[128,5376]{1,0:T(8,128)(2,1)} %collective-permute-done.5), channel_id=1, source_target_pairs={{0,120},{8,0},{16,8},{24,16},{32,24},{40,32},{48,40},{56,48},{64,5... | collective-permute-start | bytes 4128776 | tf_op jit(solution)/shard_map/ppermute | solution.py:28
  192.4 18.9 %collective-permute-start.8 = (bf16[128,5376]{1,0:T(8,128)(2,1)S(1)}, bf16[128,5376]{1,0:T(8,128)(2,1)S(1)}, u32[]{:S(2)}, u32[]{:S(2)}) collective-permute-start(bf16[128,5376]{1,0:T(8,128)(2,1)S(1)} %collective-permute-done.6), channel_id=1, source_target_pairs={{0,8},{8,16},{16,24},{24,32},{32,40},{40,48},{48,56},{56,64},{64,7... | collective-permute-start | bytes 4128776 | tf_op jit(solution)/shard_map/ppermute | solution.py:25
  192.4 18.9 %collective-permute-start.9 = (bf16[128,5376]{1,0:T(8,128)(2,1)S(1)}, bf16[128,5376]{1,0:T(8,128)(2,1)S(1)}, u32[]{:S(2)}, u32[]{:S(2)}) collective-permute-start(bf16[128,5376]{1,0:T(8,128)(2,1)S(1)} %collective-permute-done.7), channel_id=1, source_target_pairs={{0,120},{8,0},{16,8},{24,16},{32,24},{40,32},{48,40},{56,48},{64,5... | collective-permute-start | bytes 4128776 | tf_op jit(solution)/shard_map/ppermute | solution.py:28
  211.3 18.9 %collective-permute-start.10 = (bf16[128,5376]{1,0:T(8,128)(2,1)S(1)}, bf16[128,5376]{1,0:T(8,128)(2,1)S(1)}, u32[]{:S(2)}, u32[]{:S(2)}) collective-permute-start(bf16[128,5376]{1,0:T(8,128)(2,1)S(1)} %collective-permute-done.8), channel_id=1, source_target_pairs={{0,8},{8,16},{16,24},{24,32},{32,40},{40,48},{48,56},{56,64},{64,7... | collective-permute-start | bytes 4128776 | tf_op jit(solution)/shard_map/ppermute | solution.py:25
  211.3 18.9 %collective-permute-start.11 = (bf16[128,5376]{1,0:T(8,128)(2,1)S(1)}, bf16[128,5376]{1,0:T(8,128)(2,1)S(1)}, u32[]{:S(2)}, u32[]{:S(2)}) collective-permute-start(bf16[128,5376]{1,0:T(8,128)(2,1)S(1)} %collective-permute-done.9), channel_id=1, source_target_pairs={{0,120},{8,0},{16,8},{24,16},{32,24},{40,32},{48,40},{56,48},{64,5... | collective-permute-start | bytes 4128776 | tf_op jit(solution)/shard_map/ppermute | solution.py:28
  230.3 18.9 %collective-permute-start.12 = (bf16[128,5376]{1,0:T(8,128)(2,1)S(1)}, bf16[128,5376]{1,0:T(8,128)(2,1)S(1)}, u32[]{:S(2)}, u32[]{:S(2)}) collective-permute-start(bf16[128,5376]{1,0:T(8,128)(2,1)S(1)} %collective-permute-done.10), channel_id=1, source_target_pairs={{0,8},{8,16},{16,24},{24,32},{32,40},{40,48},{48,56},{56,64},{64,7... | collective-permute-start | bytes 4128776 | tf_op jit(solution)/shard_map/ppermute | solution.py:25
  230.3 18.9 %collective-permute-start.13 = (bf16[128,5376]{1,0:T(8,128)(2,1)S(1)}, bf16[128,5376]{1,0:T(8,128)(2,1)S(1)}, u32[]{:S(2)}, u32[]{:S(2)}) collective-permute-start(bf16[128,5376]{1,0:T(8,128)(2,1)S(1)} %collective-permute-done.11), channel_id=1, source_target_pairs={{0,120},{8,0},{16,8},{24,16},{32,24},{40,32},{48,40},{56,48},{64,5... | collective-permute-start | bytes 4128776 | tf_op jit(solution)/shard_map/ppermute | solution.py:28
  249.2 18.9 %collective-permute-start.14 = (bf16[128,5376]{1,0:T(8,128)(2,1)S(1)}, bf16[128,5376]{1,0:T(8,128)(2,1)S(1)}, u32[]{:S(2)}, u32[]{:S(2)}) collective-permute-start(bf16[128,5376]{1,0:T(8,128)(2,1)S(1)} %collective-permute-done.12), channel_id=1, source_target_pairs={{0,8},{8,16},{16,24},{24,32},{32,40},{40,48},{48,56},{56,64},{64,7... | collective-permute-start | bytes 4128776 | tf_op jit(solution)/shard_map/ppermute | solution.py:25
  249.2 18.9 %collective-permute-start.15 = (bf16[128,5376]{1,0:T(8,128)(2,1)S(1)}, bf16[128,5376]{1,0:T(8,128)(2,1)S(1)}, u32[]{:S(2)}, u32[]{:S(2)}) collective-permute-start(bf16[128,5376]{1,0:T(8,128)(2,1)S(1)} %collective-permute-done.13), channel_id=1, source_target_pairs={{0,120},{8,0},{16,8},{24,16},{32,24},{40,32},{48,40},{56,48},{64,5... | collective-permute-start | bytes 4128776 | tf_op jit(solution)/shard_map/ppermute | solution.py:28
  268.2 18.9 %collective-permute-start.16 = (bf16[128,5376]{1,0:T(8,128)(2,1)S(1)}, bf16[128,5376]{1,0:T(8,128)(2,1)S(1)}, u32[]{:S(2)}, u32[]{:S(2)}) collective-permute-start(bf16[128,5376]{1,0:T(8,128)(2,1)S(1)} %collective-permute-done.14), channel_id=1, source_target_pairs={{0,8},{8,16},{16,24},{24,32},{32,40},{40,48},{48,56},{56,64},{64,7... | collective-permute-start | bytes 4128776 | tf_op jit(solution)/shard_map/ppermute | solution.py:25
  268.2 20.1 %collective-permute-start.17 = (bf16[128,5376]{1,0:T(8,128)(2,1)S(1)}, bf16[128,5376]{1,0:T(8,128)(2,1)S(1)}, u32[]{:S(2)}, u32[]{:S(2)}) collective-permute-start(bf16[128,5376]{1,0:T(8,128)(2,1)S(1)} %collective-permute-done.15), channel_id=1, source_target_pairs={{0,120},{8,0},{16,8},{24,16},{32,24},{40,32},{48,40},{56,48},{64,5... | collective-permute-start | bytes 4128776 | tf_op jit(solution)/shard_map/ppermute | solution.py:28
  287.1 18.9 %collective-permute-start.18 = (bf16[128,5376]{1,0:T(8,128)(2,1)S(1)}, bf16[128,5376]{1,0:T(8,128)(2,1)S(1)}, u32[]{:S(2)}, u32[]{:S(2)}) collective-permute-start(bf16[128,5376]{1,0:T(8,128)(2,1)S(1)} %collective-permute-done.16), channel_id=1, source_target_pairs={{0,8},{8,16},{16,24},{24,32},{32,40},{40,48},{48,56},{56,64},{64,7... | collective-permute-start | bytes 4128776 | tf_op jit(solution)/shard_map/ppermute | solution.py:25
  307.3 11.0 %copy-start.7 = (f32[5376]{0:T(1024)S(1)}, f32[5376]{0:T(1024)}, u32[]{:S(2)}) copy-start(f32[5376]{0:T(1024)} %param.13) | copy-start | bytes 64516
  307.3 13.1 %copy-start.1 = (bf16[256,5376]{1,0:T(8,128)(2,1)S(1)}, bf16[256,5376]{1,0:T(8,128)(2,1)}, u32[]{:S(2)}) copy-start(bf16[256,5376]{1,0:T(8,128)(2,1)} %param.12) | copy-start | bytes 8257540
Sparse Core Ops, SparseCore 0:
  27.5 53.5 all-gather.1
